TPU v7x, 32 devices: a whole 2x2x4 slice. The times are simulated.
32 devices in a mesh: dp: 4 (over z), seq: 8 (over y, x, core).
Axes of the slice: x: 2, y: 2, z: 4, core: 2. Of those that a mesh axis runs over, the one named last changes fastest.
Arguments:
- tokens: int32 [4, 4096], P('dp', 'seq'), may hold values from 0 to 3
- embed_table: bfloat16 [4, 768], replicated, may hold values from -6 to 6
- mix_weight: bfloat16 [2, 768, 768], replicated, may hold values from -0.21875 to 0.21875
- kernels: bfloat16 [2, 3, 768], replicated, may hold values from -3.5 to 3.5
- donor_proj: bfloat16 [768, 256], replicated, may hold values from -0.21875 to 0.21875
- acceptor_proj: bfloat16 [768, 256], replicated, may hold values from -0.21875 to 0.21875
- tissue_scale: float32 [4, 256], replicated, may hold values from -0.375 to 0.375
- junction_dest: int32 [4, 2048, 1], P('dp', 'seq'), may hold values from 0 to 7; in each aligned block of 256 rows (0 to 255, 256 to 511, ..., all dimensions but the last counted through in order) at most 64 rows name the same one
- donor_offset: int32 [4, 2048], P('dp', 'seq'), may hold values from 0 to 511
- acceptor_offset: int32 [4, 2048], P('dp', 'seq'), may hold values from 0 to 511
- tissue_ids: int32 [4, 2048], P('dp', 'seq'), may hold values from 0 to 3
- targets: float32 [4, 2048], P('dp', 'seq'), may hold values from -6 to 6
Outputs:
- features: bfloat16 [4, 4096, 768], P('dp', 'seq')
- input_grad: bfloat16 [4, 4096, 768], P('dp', 'seq')
- mix_grad: float32 [2, 768, 768], P(None, 'dp')
- kernel_grad: float32 [2, 3, 768], P(None, None, 'dp')
- embed_grad: float32 [4, 768], P(None, 'dp')
- donor_grad: float32 [768, 256], P('dp')
- acceptor_grad: float32 [768, 256], P('dp')
- tissue_grad: float32 [4, 256], P(None, 'dp')
Inputs may be any that keep to these rules, and one draw needn't show every extreme that they name: `junction_dest`: in each aligned block of 256 rows (the junctions of one device) no value appears more than 64 times, a bound that some block reaches.
All inputs are finite; a program needn't handle non-finite values.
Results may differ from a plain program's by a relative error of at most 0.02.
Values may be sent and summed in bfloat16 or wider, within the bound.
A program may use at most 64 MiB of HBM per device.

v0:
```python
import jax
import jax.numpy as jnp
from jax import lax
from jax.sharding import PartitionSpec as P

FIRST_DILATION = 16
SECOND_DILATION = 128


epsilon = 1e-06


def padded(cells, sides, width):
    for axis, dim in sides:
        count = lax.axis_size(axis)
        ends = count - 1
        head = lax.slice_in_dim(cells, 0, width, axis=dim)
        tail = lax.slice_in_dim(cells, cells.shape[dim] - width, cells.shape[dim], axis=dim)
        cells = jnp.concatenate(
            [
                lax.ppermute(tail, axis, [(i, (i + 1) % count) for i in range(ends)]),
                cells,
                lax.ppermute(head, axis, [((i + 1) % count, i) for i in range(ends)]),
            ],
            axis=dim,
        )
    return cells


def normalize(stream_wide):
    inv_rms = lax.rsqrt(jnp.mean(stream_wide * stream_wide, axis=-1, keepdims=True) + epsilon)
    return (stream_wide * inv_rms, inv_rms)


def gelu_tanh(values):
    return jax.nn.gelu(values, approximate=True)


def norm_halo(norm_low, dilation):
    return padded(norm_low, (("seq", 0),), dilation)


def grad_halo(conv_low, dilation):
    return padded(conv_low, (("seq", 0),), dilation)


def per_device(
    tokens,
    embed_table,
    mix_weight,
    kernels,
    donor_proj,
    acceptor_proj,
    tissue_scale,
    junction_dest,
    donor_offset,
    acceptor_offset,
    tissue_ids,
    targets,
):
    length = tokens.shape[1]
    tok_row = tokens[0]
    vocab_hits = tok_row[:, None] == jnp.arange(embed_table.shape[0], dtype=jnp.int32)[None, :]
    stream = jnp.dot(
        vocab_hits.astype(jnp.bfloat16), embed_table, preferred_element_type=jnp.float32
    ).astype(jnp.bfloat16)
    dilation_sizes = (FIRST_DILATION, SECOND_DILATION)
    saved = []
    for layer_index in range(2):
        dilation = dilation_sizes[layer_index]
        stream_wide = stream.astype(jnp.float32)
        normed, inv_rms = normalize(stream_wide)
        norm_low = normed.astype(jnp.bfloat16)
        padded_input = norm_halo(norm_low, dilation)
        padded_wide = padded_input.astype(jnp.float32)
        kernel_wide = kernels[layer_index].astype(jnp.float32)
        conv_out = (
            kernel_wide[0] * padded_wide[:length]
            + kernel_wide[1] * padded_wide[dilation : dilation + length]
            + kernel_wide[2] * padded_wide[2 * dilation :]
        )
        activated = gelu_tanh(conv_out).astype(jnp.bfloat16)
        updated_params = stream_wide + jnp.dot(
            activated, mix_weight[layer_index], preferred_element_type=jnp.float32
        )
        saved.append((normed, inv_rms, padded_input, conv_out, activated))
        stream = updated_params.astype(jnp.bfloat16)
    dest = junction_dest[0, :, 0]
    donor_rows = donor_offset[0]
    accept_rows = acceptor_offset[0]
    tissue_row = tissue_ids[0]
    count = lax.axis_size("seq")
    capacity = 2 * dest.shape[0] // count
    dest_hits = (dest[:, None] == jnp.arange(count, dtype=jnp.int32)[None, :]).astype(jnp.int32)
    before = jnp.cumsum(dest_hits, axis=0) - dest_hits
    slot = jnp.sum(before * dest_hits, axis=1)
    request = jnp.full((count, capacity), -1, jnp.int32).at[dest, slot].set(accept_rows)
    asked = lax.all_to_all(request, "seq", split_axis=0, concat_axis=0, tiled=True)
    valid = (asked >= 0).reshape(-1)
    asked_rows = jnp.where(valid, asked.reshape(-1), 0)
    accepted = stream[asked_rows]
    accept_emb = jnp.dot(accepted, acceptor_proj, preferred_element_type=jnp.float32)
    answer = (
        jnp.where(valid[:, None], accept_emb, 0.0).astype(jnp.bfloat16).reshape(count, capacity, -1)
    )
    returned = lax.all_to_all(answer, "seq", split_axis=0, concat_axis=0, tiled=True)
    accept_wide = returned[dest, slot].astype(jnp.float32)
    donors = stream[donor_rows]
    donor_emb = jnp.dot(donors, donor_proj, preferred_element_type=jnp.float32)
    tissue_hits = (
        tissue_row[:, None] == jnp.arange(tissue_scale.shape[0], dtype=jnp.int32)[None, :]
    ).astype(jnp.float32)
    tissue_rows = jnp.dot(tissue_hits, tissue_scale, precision=lax.Precision.HIGHEST)
    score = jnp.sum(donor_emb * accept_wide * tissue_rows, axis=-1)
    misfit = score - targets[0]
    donor_back = (misfit[:, None] * accept_wide * tissue_rows).astype(jnp.bfloat16)
    accept_back = (misfit[:, None] * donor_emb * tissue_rows).astype(jnp.bfloat16)
    tissue_part = jnp.dot(
        tissue_hits.T, misfit[:, None] * donor_emb * accept_wide, precision=lax.Precision.HIGHEST
    )
    donor_part = jnp.dot(donors.T, donor_back, preferred_element_type=jnp.float32)
    back_buffer = (
        jnp.zeros((count, capacity, accept_back.shape[1]), jnp.bfloat16)
        .at[dest, slot]
        .set(accept_back)
    )
    accept_grads = lax.all_to_all(
        back_buffer, "seq", split_axis=0, concat_axis=0, tiled=True
    ).reshape(count * capacity, -1)
    accept_part = jnp.dot(accepted.T, accept_grads, preferred_element_type=jnp.float32)
    upstream = jnp.zeros((length, stream.shape[1]), jnp.float32)
    upstream = upstream.at[donor_rows].add(
        jnp.dot(donor_back, donor_proj.T, preferred_element_type=jnp.float32)
    )
    upstream = upstream.at[asked_rows].add(
        jnp.dot(accept_grads, acceptor_proj.T, preferred_element_type=jnp.float32)
    )
    mix_parts = [None, None]
    kernel_parts = [None, None]
    for layer_index in (1, 0):
        dilation = dilation_sizes[layer_index]
        normed, inv_rms, stored, conv_out, activated = saved[layer_index]
        upstream_low = upstream.astype(jnp.bfloat16)
        mix_parts[layer_index] = jnp.dot(
            activated.T, upstream_low, preferred_element_type=jnp.float32
        )
        act_grad = jnp.dot(
            upstream_low, mix_weight[layer_index].T, preferred_element_type=jnp.float32
        )
        gelu_value, pullback = jax.vjp(gelu_tanh, conv_out)
        conv_low = pullback(act_grad)[0].astype(jnp.bfloat16)
        padded_wide = stored.astype(jnp.float32)
        grad_padded = grad_halo(conv_low, dilation).astype(jnp.float32)
        conv_wide = grad_padded[dilation : dilation + length]
        kernel_parts[layer_index] = jnp.stack(
            [
                jnp.sum(conv_wide * padded_wide[:length], axis=0),
                jnp.sum(conv_wide * padded_wide[dilation : dilation + length], axis=0),
                jnp.sum(conv_wide * padded_wide[2 * dilation :], axis=0),
            ]
        )
        kernel_wide = kernels[layer_index].astype(jnp.float32)
        norm_grad = (
            kernel_wide[0] * grad_padded[2 * dilation :]
            + kernel_wide[1] * conv_wide
            + kernel_wide[2] * grad_padded[:length]
        )
        upstream = upstream + inv_rms * (
            norm_grad - normed * jnp.mean(norm_grad * normed, axis=-1, keepdims=True)
        )
    embed_part = jnp.dot(
        vocab_hits.astype(jnp.float32).T, upstream, precision=lax.Precision.HIGHEST
    )
    mix_local = jnp.stack(mix_parts)
    kernel_local = jnp.stack(kernel_parts)
    summed_output = lax.psum(
        (mix_local, donor_part, accept_part, kernel_local, embed_part, tissue_part), "seq"
    )
    mix_grad, donor_grad, accept_grad, kernel_grad, embed_grad, tissue_grad = (
        lax.psum_scatter(summed_output[0], "dp", scatter_dimension=1, tiled=True),
        lax.psum_scatter(summed_output[1], "dp", scatter_dimension=0, tiled=True),
        lax.psum_scatter(summed_output[2], "dp", scatter_dimension=0, tiled=True),
        lax.psum_scatter(summed_output[3], "dp", scatter_dimension=2, tiled=True),
        lax.psum_scatter(summed_output[4], "dp", scatter_dimension=1, tiled=True),
        lax.psum_scatter(summed_output[5], "dp", scatter_dimension=1, tiled=True),
    )
    features = stream[None]
    input_grad = upstream.astype(jnp.bfloat16)[None]
    return (
        features,
        input_grad,
        mix_grad,
        kernel_grad,
        embed_grad,
        donor_grad,
        accept_grad,
        tissue_grad,
    )


def solution(mesh):
    placed = (
        P("dp", "seq"),
        P(),
        P(),
        P(),
        P(),
        P(),
        P(),
        P("dp", "seq", None),
        P("dp", "seq"),
        P("dp", "seq"),
        P("dp", "seq"),
        P("dp", "seq"),
    )
    return jax.shard_map(
        per_device,
        mesh=mesh,
        in_specs=placed,
        out_specs=(
            P("dp", "seq", None),
            P("dp", "seq", None),
            P(None, "dp", None),
            P(None, None, "dp"),
            P(None, "dp"),
            P("dp", None),
            P("dp", None),
            P(None, "dp"),
        ),
        check_vma=False,
    )
```

profile of v0, /device:TPU:0, one launch (start us, length us, event | category | flops | bytes accessed | tf_op | source)
XLA Modules:
  0.0 411.5 jit_solution(10690004892929086083)
XLA Ops:
  10.8 38.7 %scatter_fusion = s32[8,64]{1,0:T(8,128)} fusion(s32[8,64]{1,0:T(8,128)} %broadcast_in_dim.26, s32[256]{0:T(256)S(1)} %bitcast.85, s32[256]{0:T(256)} %bitcast.103), kind=kCustom, calls=%fused_computation.3 | custom fusion | bytes 5120 | tf_op jit(solution)/shard_map/scatter | solution.py:97
  49.5 5.3 %all-to-all-start = ((s32[8,1,64]{2,1,0:T(1,128)}), s32[8,1,64]{2,1,0:T(1,128)S(1)}, u32[]{:S(2)}, u32[]{:S(2)}) async-start(s32[8,1,64]{2,1,0:T(1,128)} %bitcast.15), calls=%async_computation | async-start | bytes 8192 | tf_op jit(solution)/shard_map/all_to_all | solution.py:98
  55.6 2.4 collective-permute-start
  66.8 4.5 %collective-permute-start.2 = (bf16[128,768]{1,0:T(8,128)(2,1)S(1)}, bf16[128,768]{1,0:T(8,128)(2,1)S(1)}, u32[]{:S(2)}, u32[]{:S(2)}) collective-permute-start(bf16[128,768]{1,0:T(8,128)(2,1)S(1)} %get-tuple-element.64), channel_id=1, source_target_pairs={{0,1},{1,2},{2,3},{3,4},{4,5},{5,6},{6,7},{8,9},{9,10},{10,11},{11... | collective-permute-start | bytes 589832 | tf_op jit(solution)/shard_map/ppermute | solution.py:21
  72.7 1.9 collective-permute-done.3
  80.0 2.0 gather_fusion.1
  83.1 7.9 %all-to-all-start.1 = ((bf16[8,64,256]{2,1,0:T(8,128)(2,1)}), bf16[8,64,256]{2,1,0:T(8,128)(2,1)S(1)}, u32[]{:S(2)}, u32[]{:S(2)}) async-start(bf16[8,64,256]{2,1,0:T(8,128)(2,1)} %bitcast.17), calls=%async_computation.1 | async-start | bytes 524288 | tf_op jit(solution)/shard_map/all_to_all | solution.py:106
  92.4 5.6 %all-to-all-done.1 = bf16[8,64,256]{2,1,0:T(8,128)(2,1)S(1)} async-done(((bf16[8,64,256]{2,1,0:T(8,128)(2,1)}), bf16[8,64,256]{2,1,0:T(8,128)(2,1)S(1)}, u32[]{:S(2)}, u32[]{:S(2)}) %all-to-all-start.1) | async-done | bytes 262176 | tf_op jit(solution)/shard_map/all_to_all | solution.py:106
  98.0 1.7 gather_fusion.2
  102.3 29.6 %scatter_fusion.1 = bf16[8,64,256]{2,1,0:T(8,128)(2,1)} fusion(bf16[8,64,256]{2,1,0:T(8,128)(2,1)} %broadcast_in_dim.29, s32[256]{0:T(256)S(1)} %bitcast.86, bf16[256,256]{1,0:T(8,128)(2,1)S(1)} %copy.30), kind=kCustom, calls=%fused_computation.5 | custom fusion | bytes 395264 | tf_op jit(solution)/shard_map/scatter | solution.py:125
  131.9 4.0 all-to-all-start.2
  137.4 3.2 scatter_custom_fusion.1
  140.6 2.3 all-to-all-done.2
  142.9 2.6 fusion.84
  145.5 5.4 %scatter_fusion.2 = f32[512,768]{1,0:T(8,128)S(1)} fusion(f32[512,768]{1,0:T(8,128)S(1)} %scatter_custom_fusion.1, s32[512]{0:T(512)} %bitcast.93, f32[512,768]{1,0:T(8,128)} %fusion.84), kind=kCustom, calls=%fused_computation.6 | custom fusion | flops 393216 | bytes 4720640 | tf_op jit(solution)/shard_map/scatter-add | solution.py:135
  150.9 3.3 fusion.27
  155.8 2.0 collective-permute-start.4
  159.1 2.3 fusion.86
  161.4 2.5 convolution_bitcast_fusion
  170.0 2.4 pad_maximum_fusion
  173.9 2.8 fusion.20
  176.7 3.5 collective-permute-start.6
  188.4 2.5 convolution_bitcast_fusion.2
  192.2 2.5 reshape.248
  194.8 79.4 %reduce-scatter.13.cloned.1.call-done = f32[2,192,768]{2,1,0:T(8,128)} async-done(((f32[2,768,768]{2,1,0:T(8,128)}), f32[2,192,768]{2,1,0:T(8,128)}) %reduce-scatter.13.cloned.1.call-update) | async-done | bytes 1179664 | tf_op jit(solution)/shard_map/reduce_scatter | solution.py:180
  274.2 22.3 %reduce-scatter.23.cloned.1.call-done = f32[64,4]{1,0:T(8,128)} async-done(((f32[256,4]{1,0:T(8,128)}), f32[64,4]{1,0:T(8,128)}) %reduce-scatter.23.cloned.1.call-update) | async-done | bytes 1040
  297.4 2.4 convert_bitcast_fusion
  299.8 17.7 %reduce-scatter.21.cloned.1.call-done = f32[192,4]{1,0:T(8,128)} async-done(((f32[768,4]{1,0:T(8,128)}), f32[192,4]{1,0:T(8,128)}) %reduce-scatter.21.cloned.1.call-update) | async-done | bytes 3088
  318.5 20.7 %reduce-scatter.19.cloned.1.call-done = f32[192,6]{1,0:T(8,128)} async-done(((f32[768,6]{1,0:T(8,128)}), f32[192,6]{1,0:T(8,128)}) %reduce-scatter.19.cloned.1.call-update) | async-done | bytes 4624
  340.4 23.4 %all-reduce = (f32[2,3,192]{2,1,0:T(4,128)S(1)}, f32[4,192]{1,0:T(4,128)}, f32[4,64]{1,0:T(4,128)}) all-reduce(f32[2,3,192]{2,1,0:T(4,128)S(1)} %copy.33, f32[4,192]{1,0:T(4,128)S(1)} %copy.35, f32[4,64]{1,0:T(4,128)S(1)} %copy.37), channel_id=1, replica_groups=mesh['dp'=4,'seq'=8] {'seq'}, use_global_device_ids=true, to_apply=%region_20.21 | all-reduce | flops 2176 | bytes 17408 | tf_op jit(solution)/shard_map/psum | solution.py:176
  364.4 36.5 %all-reduce.4.cloned.1.call-done = (f32[2,192,768]{2,1,0:T(8,128)}, f32[192,256]{1,0:T(8,128)}, f32[192,256]{1,0:T(8,128)}) async-done(((f32[2,192,768]{2,1,0:T(8,128)}, f32[192,256]{1,0:T(8,128)}, f32[192,256]{1,0:T(8,128)}), (f32[2,192,768]{2,1,0:T(8,128)}, f32[192,256]{1,0:T(8,128)}, f32[192,256]{1,0:T(8,128)})) %all-reduce.4.cloned.1.call-update) | async-done | bytes 1572880 | tf_op jit(solution)/shard_map/psum | solution.py:176
  400.9 2.4 copy.44
  (201 shorter events, 50.8 us)
Async XLA Ops:
  7.2 74.8 %copy-start = (bf16[768,256]{1,0:T(8,128)(2,1)S(1)}, bf16[768,256]{1,0:T(8,128)(2,1)}, u32[]{:S(2)}) copy-start(bf16[768,256]{1,0:T(8,128)(2,1)} %param.17) | copy-start | bytes 1179652
  7.2 47.7 %copy-start.50 = (bf16[4,768]{1,0:T(4,128)(2,1)S(1)}, bf16[4,768]{1,0:T(4,128)(2,1)}, u32[]{:S(2)}) copy-start(bf16[4,768]{1,0:T(4,128)(2,1)} %param.13) | copy-start | bytes 18436
  7.2 47.7 %copy-start.44 = (s32[1,512]{1,0:T(1,128)S(1)}, s32[1,512]{1,0:T(1,128)}, u32[]{:S(2)}) copy-start(s32[1,512]{1,0:T(1,128)} %param.12) | copy-start | bytes 6148
  49.5 9.8 %copy-start.28 = (bf16[2,3,768]{2,0,1:T(2,128)(2,1)S(1)}, bf16[2,3,768]{2,0,1:T(2,128)(2,1)}, u32[]{:S(2)}) copy-start(bf16[2,3,768]{2,0,1:T(2,128)(2,1)} %param.15) | copy-start | bytes 27652
  49.5 10.0 %all-to-all-start = ((s32[8,1,64]{2,1,0:T(1,128)}), s32[8,1,64]{2,1,0:T(1,128)S(1)}, u32[]{:S(2)}, u32[]{:S(2)}) async-start(s32[8,1,64]{2,1,0:T(1,128)} %bitcast.15), calls=%async_computation | async-start | bytes 8192 | tf_op jit(solution)/shard_map/all_to_all | solution.py:98
  55.6 5.2 %collective-permute-start = (bf16[16,768]{1,0:T(8,128)(2,1)S(1)}, bf16[16,768]{1,0:T(8,128)(2,1)S(1)}, u32[]{:S(2)}, u32[]{:S(2)}) collective-permute-start(bf16[16,768]{1,0:T(8,128)(2,1)S(1)} %get-tuple-element.66), channel_id=1, source_target_pairs={{0,1},{1,2},{2,3},{3,4},{4,5},{5,6},{6,7},{8,9},{9,10},{10,11},{11... | collective-permute-start | bytes 73736 | tf_op jit(solution)/shard_map/ppermute | solution.py:21
  58.0 4.2 %collective-permute-start.1 = (bf16[16,768]{1,0:T(8,128)(2,1)S(1)}, bf16[16,768]{1,0:T(8,128)(2,1)S(1)}, u32[]{:S(2)}, u32[]{:S(2)}) collective-permute-start(bf16[16,768]{1,0:T(8,128)(2,1)S(1)} %get-tuple-element.67), channel_id=1, source_target_pairs={{1,0},{2,1},{3,2},{4,3},{5,4},{6,5},{7,6},{9,8},{10,9},{11,10},{12... | collective-permute-start | bytes 73736 | tf_op jit(solution)/shard_map/ppermute | solution.py:23
  59.4 15.3 %copy-start.29 = (f32[768]{0:T(1024)}, f32[768]{0:T(1024)S(1)}, u32[]{:S(2)}) copy-start(f32[768]{0:T(1024)S(1)} %get-tuple-element.38) | copy-start | bytes 9220
  59.4 15.3 %copy-start.31 = (f32[768]{0:T(1024)}, f32[768]{0:T(1024)S(1)}, u32[]{:S(2)}) copy-start(f32[768]{0:T(1024)S(1)} %get-tuple-element.39) | copy-start | bytes 9220
  59.4 15.3 %copy-start.33 = (f32[768]{0:T(1024)}, f32[768]{0:T(1024)S(1)}, u32[]{:S(2)}) copy-start(f32[768]{0:T(1024)S(1)} %get-tuple-element.40) | copy-start | bytes 9220
  60.8 11.9 %copy-start.37 = (s32[512,1]{0,1:T(1,128)}, s32[512,1]{0,1:T(1,128)S(1)}, u32[]{:S(2)}) copy-start(s32[512,1]{0,1:T(1,128)S(1)} %compare_select_fusion) | copy-start | bytes 6148
  65.9 99.5 %copy-start.13 = (bf16[512,768]{1,0:T(8,128)(2,1)}, bf16[512,768]{1,0:T(8,128)(2,1)S(1)}, u32[]{:S(2)}) copy-start(bf16[512,768]{1,0:T(8,128)(2,1)S(1)} %get-tuple-element.75) | copy-start | bytes 2359300
  66.8 5.9 %collective-permute-start.2 = (bf16[128,768]{1,0:T(8,128)(2,1)S(1)}, bf16[128,768]{1,0:T(8,128)(2,1)S(1)}, u32[]{:S(2)}, u32[]{:S(2)}) collective-permute-start(bf16[128,768]{1,0:T(8,128)(2,1)S(1)} %get-tuple-element.64), channel_id=1, source_target_pairs={{0,1},{1,2},{2,3},{3,4},{4,5},{5,6},{6,7},{8,9},{9,10},{10,11},{11... | collective-permute-start | bytes 589832 | tf_op jit(solution)/shard_map/ppermute | solution.py:21
  71.2 3.3 collective-permute-start.3
  83.1 16.7 %copy-start.40 = (f32[4,256]{1,0:T(4,128)S(1)}, f32[4,256]{1,0:T(4,128)}, u32[]{:S(2)}) copy-start(f32[4,256]{1,0:T(4,128)} %param.18) | copy-start | bytes 12292
  83.1 16.7 %copy-start.41 = (s32[1,256]{1,0:T(1,128)S(1)}, s32[1,256]{1,0:T(1,128)}, u32[]{:S(2)}) copy-start(s32[1,256]{1,0:T(1,128)} %param.22) | copy-start | bytes 3076
  83.1 14.9 %all-to-all-start.1 = ((bf16[8,64,256]{2,1,0:T(8,128)(2,1)}), bf16[8,64,256]{2,1,0:T(8,128)(2,1)S(1)}, u32[]{:S(2)}, u32[]{:S(2)}) async-start(bf16[8,64,256]{2,1,0:T(8,128)(2,1)} %bitcast.17), calls=%async_computation.1 | async-start | bytes 524288 | tf_op jit(solution)/shard_map/all_to_all | solution.py:106
  91.0 103.7 %reduce-scatter.15.cloned.1.call-start = ((), (), s32[]{:S(2)}) async-start(), calls=%async_computation.10 | async-start | bytes 983040 | tf_op jit(solution)/shard_map/reduce_scatter | solution.py:181
  101.6 34.6 %copy-start.24 = (bf16[768,256]{1,0:T(8,128)(2,1)S(1)}, bf16[768,256]{1,0:T(8,128)(2,1)}, u32[]{:S(2)}) copy-start(bf16[768,256]{1,0:T(8,128)(2,1)} %param.16) | copy-start | bytes 1179652
  131.9 11.0 %all-to-all-start.2 = ((bf16[8,64,256]{2,1,0:T(8,128)(2,1)}), bf16[8,64,256]{2,1,0:T(8,128)(2,1)}, u32[]{:S(2)}, u32[]{:S(2)}) async-start(bf16[8,64,256]{2,1,0:T(8,128)(2,1)} %scatter_fusion.1), calls=%async_computation.2 | async-start | bytes 524288 | tf_op jit(solution)/shard_map/all_to_all | solution.py:127
  136.0 58.8 %reduce-scatter.17.cloned.1.call-start = ((), (), s32[]{:S(2)}) async-start(), calls=%async_computation.11 | async-start | bytes 983040 | tf_op jit(solution)/shard_map/reduce_scatter | solution.py:182
  155.8 8.1 %collective-permute-start.4 = (bf16[128,768]{1,0:T(8,128)(2,1)}, bf16[128,768]{1,0:T(8,128)(2,1)}, u32[]{:S(2)}, u32[]{:S(2)}) collective-permute-start(bf16[128,768]{1,0:T(8,128)(2,1)} %get-tuple-element.62), channel_id=1, source_target_pairs={{0,1},{1,2},{2,3},{3,4},{4,5},{5,6},{6,7},{8,9},{9,10},{10,11},{11... | collective-permute-start | bytes 589832 | tf_op jit(solution)/shard_map/ppermute | solution.py:21
  157.8 6.2 %collective-permute-start.5 = (bf16[128,768]{1,0:T(8,128)(2,1)}, bf16[128,768]{1,0:T(8,128)(2,1)}, u32[]{:S(2)}, u32[]{:S(2)}) collective-permute-start(bf16[128,768]{1,0:T(8,128)(2,1)} %get-tuple-element.63), channel_id=1, source_target_pairs={{1,0},{2,1},{3,2},{4,3},{5,4},{6,5},{7,6},{9,8},{10,9},{11,10},{12... | collective-permute-start | bytes 589832 | tf_op jit(solution)/shard_map/ppermute | solution.py:23
  161.4 112.8 %reduce-scatter.13.cloned.1.call-start = ((), (), s32[]{:S(2)}) async-start(), calls=%async_computation.9 | async-start | bytes 5898240 | tf_op jit(solution)/shard_map/reduce_scatter | solution.py:180
  172.5 124.1 %reduce-scatter.23.cloned.1.call-start = ((), (), s32[]{:S(2)}) async-start(), calls=%async_computation.14 | async-start | bytes 163840
  176.7 8.2 %collective-permute-start.6 = (bf16[16,768]{1,0:T(8,128)(2,1)S(1)}, bf16[16,768]{1,0:T(8,128)(2,1)S(1)}, u32[]{:S(2)}, u32[]{:S(2)}) collective-permute-start(bf16[16,768]{1,0:T(8,128)(2,1)S(1)} %get-tuple-element.60), channel_id=1, source_target_pairs={{0,1},{1,2},{2,3},{3,4},{4,5},{5,6},{6,7},{8,9},{9,10},{10,11},{11... | collective-permute-start | bytes 73736 | tf_op jit(solution)/shard_map/ppermute | solution.py:21
  180.2 4.6 %collective-permute-start.7 = (bf16[16,768]{1,0:T(8,128)(2,1)S(1)}, bf16[16,768]{1,0:T(8,128)(2,1)S(1)}, u32[]{:S(2)}, u32[]{:S(2)}) collective-permute-start(bf16[16,768]{1,0:T(8,128)(2,1)S(1)} %get-tuple-element.61), channel_id=1, source_target_pairs={{1,0},{2,1},{3,2},{4,3},{5,4},{6,5},{7,6},{9,8},{10,9},{11,10},{12... | collective-permute-start | bytes 73736 | tf_op jit(solution)/shard_map/ppermute | solution.py:23
  182.7 134.8 %reduce-scatter.21.cloned.1.call-start = ((), (), s32[]{:S(2)}) async-start(), calls=%async_computation.13 | async-start | bytes 491520
  190.9 148.3 %reduce-scatter.19.cloned.1.call-start = ((), (), s32[]{:S(2)}) async-start(), calls=%async_computation.12 | async-start | bytes 491520
  192.2 105.2 %copy-start.7 = (f32[512,768]{1,0:T(8,128)S(1)}, f32[512,768]{1,0:T(8,128)}, u32[]{:S(2)}) copy-start(f32[512,768]{1,0:T(8,128)} %copy-done.6) | copy-start | bytes 4718596
  192.2 105.2 %copy-start.10 = (f32[512,768]{1,0:T(8,128)S(1)}, f32[512,768]{1,0:T(8,128)}, u32[]{:S(2)}) copy-start(f32[512,768]{1,0:T(8,128)} %copy-done.8) | copy-start | bytes 4718596
  194.7 206.2 %all-reduce.4.cloned.1.call-start = ((), (), s32[]{:S(2)}) async-start(), calls=%async_computation.15 | async-start | bytes 3145728 | tf_op jit(solution)/shard_map/psum | solution.py:176
  (37 other events, 129.4 us)
Sparse Core Ops, SparseCore 0:
  101.6 22.9 reduce-scatter.14
  161.5 25.8 reduce-scatter.16
  189.6 84.5 reduce-scatter.12
  276.9 19.6 reduce-scatter.22
  298.8 18.7 reduce-scatter.20
  320.3 18.8 reduce-scatter.18
  343.0 57.7 all-reduce.3
where the time goes:
time: 414 us; the launch traced here: 411 us
  waiting for transfers between devices  188 us (45%)
  local copies, waits for them, and re-layouts  98.6 us (24%)
  starting transfers between devices  35.4 us (9%)
  matrix products  25.8 us (6%)
  other arithmetic  25.1 us (6%)
  blocking collectives  23.4 us (6%)
  between operations  15.1 us (4%)
    reduce_scatter x1, waiting for transfers between devices, per_device(): lax.psum_scatter(summed_output[0], 'dp', scatter_dimension=1, tiled=True)  79.4 us
    unnamed x10, waiting for transfers between devices  60.9 us
    scatter x1, local copies, waits for them, and re-layouts, per_device(): jnp.full((count, capacity), -1, jnp.int32).at[dest, slot].set(accept_rows)  38.7 us
    psum x1, waiting for transfers between devices, per_device(): lax.psum((mix_local, donor_part, accept_part, kernel_local, embed_part, t...  36.5 us
    scatter x1, local copies, waits for them, and re-layouts, per_device(): back_buffer = jnp.zeros((count, capacity, accept_back.shape[1]), jnp.bflo...  29.6 us
    psum x1, blocking collectives, per_device(): lax.psum((mix_local, donor_part, accept_part, kernel_local, embed_part, t...  23.4 us
    unnamed x112, local copies, waits for them, and re-layouts  20.1 us
    ppermute x4, starting transfers between devices, padded(): lax.ppermute(tail, axis, [(i, (i + 1) % count) for i in range(ends)])  12.3 us
  transfers between devices with their start and end apart: 18, of which 9 were waited for; matrix products, arithmetic and copies ran while one was open for 20% of the time, Pallas kernels for 0%

commit v1 on v0

v1 whole, which is shorter than its diff:
```python
import functools
import math

import jax
import jax.numpy as jnp
from jax import lax
from jax.experimental import pallas as pl
from jax.experimental.pallas import tpu as pltpu
from jax.sharding import PartitionSpec as P

D0 = 16
D1 = 128
EPS = 1e-06
GROUP = 8
COMBOS = 128
ROOT = math.sqrt(2.0 / math.pi)
CUBE = 0.044715
F32 = jnp.float32
BF16 = jnp.bfloat16
MESH = pl.DeviceIdType.MESH


def mm(a, b):
    return lax.dot_general(a, b, (((1,), (0,)), ((), ())), preferred_element_type=F32)


def mm_ta(a, b):
    return lax.dot_general(a, b, (((0,), (0,)), ((), ())), preferred_element_type=F32)


def mm_tb(a, b):
    return lax.dot_general(a, b, (((1,), (1,)), ((), ())), preferred_element_type=F32)


def onehot(cond):
    return jnp.where(cond, 1.0, 0.0).astype(BF16)


def gelu_and_slope(v):
    square = v * v
    t = jnp.tanh(ROOT * (v + CUBE * (square * v)))
    half = 0.5 * (1.0 + t)
    slope = half + (0.5 * ROOT) * v * (1.0 - t * t) * (1.0 + (3.0 * CUBE) * square)
    return v * half, slope


def body(dims, *refs):
    n, m, L, J, C, E, cap, V = dims
    (tok, emb, mix, kern, dproj, aproj, tscale, dest, doff, aoff, tissue, targets) = refs[:12]
    (feat, igrad, mixg, kerng, embg, dong, accg, tisg) = refs[12:20]
    (info_src, info_all, x1, n1e, act, gp1, G, Dm, ans, ret, bb, gq, A, g2, da, dc1e, g1, dc0e,
     gp0, n0l, n0c, n0r, acttT, mt, oh, ohT, n0g, gp0g, inv0g,
     pay, rc, chip, rj, ck, rz, F, sp, rs, s1, rsz, sall, ssem, rsem) = refs[20:]
    me = lax.axis_index("seq")
    q = lax.axis_index("dp")
    groups = n // GROUP
    T = m * groups
    low = lax.rem(me, GROUP)
    base = me - low
    grp = me // GROUP
    b0 = lax.rem(low, 2)
    j0 = low // 2
    rows_q = C // m
    sems = [0]
    sent = []

    def send(src, dst, dp, sq):
        k = sems[0]
        sems[0] += 1
        d = pltpu.make_async_remote_copy(
            src_ref=src, dst_ref=dst, send_sem=ssem.at[k], recv_sem=rsem.at[k],
            device_id=(dp, sq), device_id_type=MESH)
        d.start()
        sent.append(d)
        return d

    def seq_peer(k):
        return lax.rem(me + k, n)

    def low_peer(k):
        return lax.rem(low + k, GROUP)

    def t_peer(k):
        t = lax.rem(q * groups + grp + k, T)
        return t // groups, lax.rem(t, groups)

    barrier = pltpu.get_barrier_semaphore()
    count = 0
    for k in range(1, n):
        pl.semaphore_signal(barrier, inc=1, device_id=(q, seq_peer(k)), device_id_type=MESH)
        count += 1
    for k in range(1, m):
        for g in range(groups):
            pl.semaphore_signal(
                barrier, inc=1,
                device_id=(lax.rem(q + k, m), g * GROUP + low), device_id_type=MESH)
            count += 1
    info_src[...] = jnp.zeros_like(info_src)
    info_src[0:1, :L] = tok[...]
    info_src[1:2, :J] = dest[...]
    info_src[1:2, J:2 * J] = aoff[...]
    info_all[me] = info_src[...]
    pl.semaphore_wait(barrier, count)
    info_cp = [send(info_src, info_all.at[me], q, seq_peer(k)) for k in range(1, n)]

    ew = emb[...].astype(F32)
    inv0 = lax.rsqrt(jnp.mean(ew * ew, axis=-1, keepdims=True) + EPS)
    norm0 = ew * inv0
    n0 = norm0.astype(BF16).astype(F32)
    k0 = kern[0].astype(F32)
    k1 = kern[1].astype(F32)
    idf = lax.broadcasted_iota(jnp.int32, (COMBOS, 1), 0).astype(F32)
    cc = jnp.floor((idf + 0.5) * (1.0 / 25.0))
    rest = idf - 25.0 * cc
    ll = jnp.floor((rest + 0.5) * 0.2)
    rr = rest - 5.0 * ll

    def pick(which, table):
        out = jnp.zeros((COMBOS, table.shape[1]), F32)
        for v in range(V):
            out = out + jnp.where(which == float(v), table[v:v + 1], 0.0)
        return out

    n0l[...] = pick(ll, n0)
    n0c[...] = pick(cc, n0)
    n0r[...] = pick(rr, n0)
    conv0 = k0[0:1] * n0l[...] + k0[1:2] * n0c[...] + k0[2:3] * n0r[...]
    a0, s0 = gelu_and_slope(conv0)
    gp0[...] = s0
    a0 = a0.astype(BF16)
    acttT[...] = a0.astype(F32).T.astype(BF16)
    x1t = (pick(cc, ew) + mm(a0, mix[0])).astype(BF16)
    xw = x1t.astype(F32)
    n1t = (xw * lax.rsqrt(jnp.mean(xw * xw, axis=-1, keepdims=True) + EPS)).astype(BF16)
    invc = pick(cc, jnp.broadcast_to(inv0, (V, 128)))
    lane = lax.broadcasted_iota(jnp.int32, (COMBOS, 128), 1)
    hi = invc.astype(BF16).astype(F32)
    invt = jnp.where(lane == 0, hi, jnp.where(lane == 1, invc - hi, 0.0)).astype(BF16)
    mt[:, :C] = x1t
    mt[:, C:2 * C] = n1t

    upper = onehot(lax.broadcasted_iota(jnp.int32, (J, J), 0) < lax.broadcasted_iota(jnp.int32, (J, J), 1))
    eye = lax.broadcasted_iota(jnp.int32, (J, J), 0) == lax.broadcasted_iota(jnp.int32, (J, J), 1)

    def col(row):
        return jnp.sum(jnp.where(eye, row, 0.0), axis=1, keepdims=True)

    mine = lax.broadcasted_iota(jnp.int32, (n, J), 0) == dest[...]
    before = mm(onehot(mine), upper)
    slot = jnp.sum(jnp.where(mine, before, 0.0), axis=0, keepdims=True)
    place = dest[...].astype(F32) * float(cap) + slot
    Dm[...] = onehot(lax.broadcasted_iota(jnp.int32, (n * cap, J), 0).astype(F32) == place)
    OHd = onehot(lax.broadcasted_iota(jnp.int32, (L, J), 0) == doff[...])
    tcol = col(tissue[...].astype(F32))
    ycol = col(targets[...])

    for cp in info_cp:
        cp.wait_recv()
    lt = jnp.where(me == 0, V, info_all[lax.rem(me + n - 1, n)][0:1, :L])
    rt = jnp.where(me == n - 1, V, info_all[lax.rem(me + 1, n)][0:1, :L])
    te = jnp.concatenate([lt[:, L - 256:], tok[...], rt[:, :256]], axis=1)
    W = L + 2 * D1
    o = 256 - D1
    cen = te[:, o:o + W]
    comb = (cen * 5 + te[:, o - D0:o - D0 + W]) * 5 + te[:, o + D0:o + D0 + W]
    comb = jnp.where(cen == V, 1000, comb)
    hot = jnp.where(lax.broadcasted_iota(jnp.int32, (COMBOS, W), 0) == comb, 1.0, 0.0)
    ohT[...] = hot.astype(BF16)
    oh[...] = hot.T.astype(BF16)

    x1[...] = mm(oh[D1:D1 + L], mt[:, :C]).astype(BF16)
    n1e[...] = mm(oh[...], mt[:, C:2 * C]).astype(BF16)

    R = 32

    @pl.loop(0, L // R)
    def _(i):
        r = pl.multiple_of(i * R, R)
        v = (k1[0:1] * n1e[pl.ds(r, R)].astype(F32) + k1[1:2] * n1e[pl.ds(r + D1, R)].astype(F32)
             + k1[2:3] * n1e[pl.ds(r + 2 * D1, R)].astype(F32))
        a, s = gelu_and_slope(v)
        act[pl.ds(r, R)] = a.astype(BF16)
        gp1[pl.ds(r, R)] = s

    for h in range(2):
        sl = slice(h * L // 2, (h + 1) * L // 2)
        feat[sl] = (x1[sl].astype(F32) + mm(act[sl], mix[1])).astype(BF16)

    rows = [info_all[s][1:2, :] for s in range(n)]
    dests = jnp.concatenate([r[:, :J] for r in rows], axis=0)
    hits = dests == me
    bef = jnp.where(hits, mm(onehot(hits), upper), -1.0)
    for s in range(n):
        pick_s = lax.broadcasted_iota(jnp.int32, (cap, J), 0).astype(F32) == bef[s:s + 1]
        offs = rows[s][:, J:2 * J].astype(F32) + 1.0
        pos = jnp.sum(jnp.where(pick_s, offs, 0.0), axis=1, keepdims=True) - 1.0
        G[s * cap:(s + 1) * cap] = onehot(
            lax.broadcasted_iota(jnp.int32, (cap, L), 1).astype(F32) == pos)
    qx = mm(feat[...], aproj[...]).astype(BF16)
    ans[...] = mm(G[...], qx).astype(BF16).reshape(n, cap, E)
    ans_cp = [send(ans.at[seq_peer(k)], ret.at[me], q, seq_peer(k)) for k in range(1, n)]
    ret[me] = ans[me]

    donors = mm_ta(OHd, feat[...]).astype(BF16)
    pd = mm(donors, dproj[...])
    trow = jnp.zeros((J, E), F32)
    for t in range(tscale.shape[0]):
        trow = trow + jnp.where(tcol == float(t), tscale[t:t + 1], 0.0)
    mid = slice(D1, D1 + L)
    n0g[...] = mm(oh[mid], n0c[...].astype(BF16)).astype(BF16)
    gp0g[...] = mm(oh[mid], gp0[...].astype(BF16)).astype(BF16)
    inv0g[...] = mm(oh[mid], invt)

    for cp in ans_cp:
        cp.wait_recv()
    qj = mm_ta(Dm[...], ret[...].reshape(n * cap, E))
    misfit = jnp.sum(pd * qj * trow, axis=-1, keepdims=True) - ycol
    dP = (misfit * qj * trow).astype(BF16)
    dQ = (misfit * pd * trow).astype(BF16)
    bb[...] = mm(Dm[...], dQ).astype(BF16).reshape(n, cap, E)
    back_cp = [send(bb.at[seq_peer(k)], gq.at[me], q, seq_peer(k)) for k in range(1, n)]
    gq[me] = bb[me]

    tg = misfit * pd * qj
    A[:, :E] = mm(OHd, dP).astype(BF16)
    sp[7] = jnp.zeros_like(sp[7])
    tail = [jnp.sum(jnp.where(tcol == float(t), tg, 0.0), axis=0, keepdims=True)
            for t in range(tscale.shape[0])]
    g2[...] = mm_tb(A[:, :E], dproj[...])

    def weights_half(h):
        a = A[:, h * E:(h + 1) * E]
        for which, left in ((0, act), (4, feat)):
            out = mm_ta(left[...], a).astype(BF16)
            for c in range(E // 128):
                pay[which + h * (E // 128) + c] = out[:, c * 128:(c + 1) * 128]

    weights_half(0)

    for cp in back_cp:
        cp.wait_recv()
    A[:, E:] = mm_ta(G[...], gq[...].reshape(n * cap, E)).astype(BF16)
    g2[...] += mm_tb(A[:, E:], aproj[...])
    da[...] = mm_tb(g2[...].astype(BF16), mix[1])

    def slope_times(i):
        r = pl.multiple_of(i * R, R)
        dc1e[pl.ds(r + D1, R)] = (da[pl.ds(r, R)] * gp1[pl.ds(r, R)]).astype(BF16)

    pl.loop(0, D1 // R)(slope_times)
    pl.loop((L - D1) // R, L // R)(slope_times)
    halo_cp = [
        send(dc1e.at[pl.ds(L, D1)], dc1e.at[pl.ds(0, D1)], q, seq_peer(1)),
        send(dc1e.at[pl.ds(D1, D1)], dc1e.at[pl.ds(L + D1, D1)], q, seq_peer(n - 1)),
    ]
    weights_half(1)
    core_cp = send(pay.at[pl.ds((1 - b0) * 4, 4)], rc, q, me + 1 - 2 * b0)
    pl.loop(D1 // R, (L - D1) // R)(slope_times)

    def kg(i, accs):
        r = pl.multiple_of(i * R, R)
        d = dc1e[pl.ds(r + D1, R)].astype(F32)
        return tuple(
            acc + jnp.sum((d * n1e[pl.ds(r + k * D1, R)].astype(F32)).reshape(R // 8, 8, C), axis=0)
            for k, acc in enumerate(accs))

    kacc = lax.fori_loop(0, L // R, kg, tuple(jnp.zeros((8, C), F32) for _ in range(3)))
    kacc = [jnp.sum(a, axis=0, keepdims=True) for a in kacc]
    zc = jnp.zeros((1, C), F32)
    tail = [jnp.concatenate([t, jnp.zeros((1, C - E), F32)], axis=1) for t in tail]
    extra = jnp.concatenate(kacc + [zc] + tail + [zc] * 8, axis=0)

    for cp in halo_cp:
        cp.wait_recv()

    @pl.when(me == 0)
    def _():
        dc1e[0:D1] = jnp.zeros((D1, C), BF16)

    @pl.when(me == n - 1)
    def _():
        dc1e[L + D1:] = jnp.zeros((D1, C), BF16)

    @pl.loop(0, L // R)
    def _(i):
        r = pl.multiple_of(i * R, R)
        dn = (k1[0:1] * dc1e[pl.ds(r + 2 * D1, R)].astype(F32)
              + k1[1:2] * dc1e[pl.ds(r + D1, R)].astype(F32)
              + k1[2:3] * dc1e[pl.ds(r, R)].astype(F32))
        xx = x1[pl.ds(r, R)].astype(F32)
        inv = lax.rsqrt(jnp.mean(xx * xx, axis=-1, keepdims=True) + EPS)
        nn = xx * inv
        g1[pl.ds(r, R)] = g2[pl.ds(r, R)] + inv * (dn - nn * jnp.mean(dn * nn, axis=-1, keepdims=True))

    S = mm(ohT[:, mid], g1[...].astype(BF16))
    for r in range(7):
        sp[r] = S[r * 16:(r + 1) * 16].astype(BF16)
    sp[7] = extra.astype(BF16)
    srs_cp = [send(sp.at[low_peer(k)], rs.at[k - 1], q, base + low_peer(k)) for k in range(1, GROUP)]

    core_cp.wait_recv()
    for j in range(4):
        chip[j] = (pay[b0 * 4 + j].astype(F32) + rc[j].astype(F32)).astype(BF16)
    chip_cp = []
    for k in range(1, 4):
        jj = lax.rem(j0 + k, 4)
        chip_cp.append(send(chip.at[jj], rj.at[k - 1], q, base + jj * 2 + b0))

    da[...] = mm_tb(g1[...].astype(BF16), mix[0])

    def slope0(i):
        r = pl.multiple_of(i * 16, 16)
        dc0e[pl.ds(r + D0, 16)] = (da[pl.ds(r, 16)] * gp0g[pl.ds(r, 16)].astype(F32)).astype(BF16)

    slope0(0)
    slope0(L // 16 - 1)
    halo0_cp = [
        send(dc0e.at[pl.ds(L, D0)], dc0e.at[pl.ds(0, D0)], q, seq_peer(1)),
        send(dc0e.at[pl.ds(D0, D0)], dc0e.at[pl.ds(L + D0, D0)], q, seq_peer(n - 1)),
    ]
    pl.loop(1, L // 16 - 1)(slope0)

    for cp in srs_cp:
        cp.wait_recv()
    tot = sp[low].astype(F32)
    for k in range(GROUP - 1):
        tot = tot + rs[k].astype(F32)
    s1[...] = tot.astype(BF16)
    sz_cp = []
    for k in range(1, T):
        pq, pg = t_peer(k)
        sz_cp.append(send(s1, rsz.at[k - 1], pq, pg * GROUP + low))

    for cp in chip_cp:
        cp.wait_recv()
    ck[...] = (chip[j0].astype(F32) + rj[0].astype(F32) + rj[1].astype(F32) + rj[2].astype(F32)).astype(BF16)
    z_cp = []
    for k in range(1, T):
        pq, pg = t_peer(k)
        z_cp.append(send(ck.at[pl.ds(pl.multiple_of(pq * rows_q, 16), rows_q)], rz.at[k - 1], pq, pg * GROUP + low))

    for cp in halo0_cp:
        cp.wait_recv()

    @pl.when(me == 0)
    def _():
        dc0e[0:D0] = jnp.zeros((D0, C), BF16)

    @pl.when(me == n - 1)
    def _():
        dc0e[L + D0:] = jnp.zeros((D0, C), BF16)

    for cp in sz_cp:
        cp.wait_recv()
    tot = s1[...].astype(F32)
    for k in range(T - 1):
        tot = tot + rsz[k].astype(F32)
    sall[low] = tot.astype(BF16)
    sag_cp = [send(sall.at[low], sall.at[low], q, base + low_peer(k)) for k in range(1, GROUP)]

    for cp in z_cp:
        cp.wait_recv()
    tot = ck[pl.ds(pl.multiple_of(q * rows_q, 16), rows_q)].astype(F32)
    for k in range(T - 1):
        tot = tot + rz[k].astype(F32)
    p0 = b0 * 4 + j0
    F[p0] = tot.astype(BF16)
    ag_cp = [send(F.at[p0], F.at[p0], q, base + low_peer(k)) for k in range(1, GROUP)]

    @pl.loop(0, L // R)
    def _(i):
        r = pl.multiple_of(i * R, R)
        dn = (k0[0:1] * dc0e[pl.ds(r + 2 * D0, R)].astype(F32)
              + k0[1:2] * dc0e[pl.ds(r + D0, R)].astype(F32)
              + k0[2:3] * dc0e[pl.ds(r, R)].astype(F32))
        nn = n0g[pl.ds(r, R)].astype(F32)
        inv = jnp.sum(inv0g[pl.ds(r, R)], axis=-1, keepdims=True)
        igrad[pl.ds(r, R)] = (
            g1[pl.ds(r, R)] + inv * (dn - nn * jnp.mean(dn * nn, axis=-1, keepdims=True))
        ).astype(BF16)

    for cp in sag_cp:
        cp.wait_recv()
    St = sall[...].reshape(COMBOS, C)
    live = lax.broadcasted_iota(jnp.int32, (COMBOS, C), 0) < 25 * V
    Sm = jnp.where(live, St.astype(F32), 0.0)
    Sb = Sm.astype(BF16)
    mixg[0] = mm(acttT[pl.ds(pl.multiple_of(q * rows_q, 16), rows_q)], Sb)
    Tm = mm_tb(Sb, mix[0]) * gp0[...]

    def own(full, part):
        w = full.shape[1] // m
        out = jnp.zeros((full.shape[0], w), F32)
        for i in range(m):
            out = out + jnp.where(q == i, full[:, i * w:(i + 1) * w], 0.0)
        return out

    kg0 = jnp.concatenate(
        [jnp.sum(t[...] * Tm, axis=0, keepdims=True) for t in (n0l, n0c, n0r)], axis=0)
    kerng[0] = own(kg0, C)
    last = sall[7].astype(F32)
    kerng[1] = own(last[0:3], C)
    tisg[...] = own(last[4:4 + tscale.shape[0], :E], E)
    eg = []
    for v in range(V):
        def total(which, x):
            return jnp.sum(jnp.where(which == float(v), x, 0.0), axis=0, keepdims=True)
        D = k0[0:1] * total(ll, Tm) + k0[1:2] * total(cc, Tm) + k0[2:3] * total(rr, Tm)
        nv = norm0[v:v + 1]
        eg.append(total(cc, Sm) + inv0[v:v + 1] * (D - nv * jnp.mean(D * nv, axis=-1, keepdims=True)))
    embg[...] = own(jnp.concatenate(eg, axis=0), C)

    for cp in ag_cp:
        cp.wait_recv()
    half = E // 128
    md = jnp.concatenate([F[i] for i in range(half)], axis=1)
    ma = jnp.concatenate([F[half + i] for i in range(half)], axis=1)
    mixg[1] = mm_tb(md, dproj[...]) + mm_tb(ma, aproj[...])
    for i in range(half):
        dong[:, i * 128:(i + 1) * 128] = F[4 + i].astype(F32)
        accg[:, i * 128:(i + 1) * 128] = F[4 + half + i].astype(F32)
    for cp in sent:
        cp.wait_send()


def per_device(tokens, embed_table, mix_weight, kernels, donor_proj, acceptor_proj, tissue_scale,
               junction_dest, donor_offset, acceptor_offset, tissue_ids, targets):
    n = lax.axis_size("seq")
    m = lax.axis_size("dp")
    L = tokens.shape[1]
    J = donor_offset.shape[1]
    V, C = embed_table.shape
    E = donor_proj.shape[1]
    cap = 2 * J // n
    groups = n // GROUP
    T = m * groups
    rq = C // m
    W = L + 2 * D1
    vm = pltpu.VMEM
    nsem = 3 * (n - 1) + 4 + 1 + 3 + 2 * (T - 1) + 3 * (GROUP - 1)
    scratch = [
        vm((8, max(L, 2 * J)), jnp.int32), vm((n, 8, max(L, 2 * J)), jnp.int32),
        vm((L, C), BF16), vm((W, C), BF16), vm((L, C), BF16), vm((L, C), F32),
        vm((n * cap, L), BF16), vm((n * cap, J), BF16),
        vm((n, cap, E), BF16), vm((n, cap, E), BF16), vm((n, cap, E), BF16), vm((n, cap, E), BF16),
        vm((L, 2 * E), BF16), vm((L, C), F32), vm((L, C), F32), vm((W, C), BF16),
        vm((L, C), F32), vm((L + 2 * D0, C), BF16),
        vm((COMBOS, C), F32), vm((COMBOS, C), F32), vm((COMBOS, C), F32), vm((COMBOS, C), F32),
        vm((C, COMBOS), BF16), vm((COMBOS, 2 * C), BF16),
        vm((W, COMBOS), BF16), vm((COMBOS, W), BF16),
        vm((L, C), BF16), vm((L, C), BF16), vm((L, 128), F32),
        vm((8, C, 128), BF16), vm((4, C, 128), BF16), vm((4, C, 128), BF16), vm((3, C, 128), BF16),
        vm((C, 128), BF16), vm((T - 1, rq, 128), BF16), vm((8, rq, 128), BF16),
        vm((8, 16, C), BF16), vm((7, 16, C), BF16), vm((16, C), BF16), vm((T - 1, 16, C), BF16),
        vm((8, 16, C), BF16),
        pltpu.SemaphoreType.DMA((nsem,)), pltpu.SemaphoreType.DMA((nsem,)),
    ]
    outs = [
        jax.ShapeDtypeStruct((L, C), BF16), jax.ShapeDtypeStruct((L, C), BF16),
        jax.ShapeDtypeStruct((2, rq, C), F32), jax.ShapeDtypeStruct((2, 3, rq), F32),
        jax.ShapeDtypeStruct((V, rq), F32), jax.ShapeDtypeStruct((rq, E), F32),
        jax.ShapeDtypeStruct((rq, E), F32), jax.ShapeDtypeStruct((tissue_scale.shape[0], E // m), F32),
    ]
    spec = pl.BlockSpec(memory_space=pltpu.VMEM)
    res = pl.pallas_call(
        functools.partial(body, (n, m, L, J, C, E, cap, V)),
        out_shape=outs,
        in_specs=[spec] * 12,
        out_specs=[spec] * 8,
        scratch_shapes=scratch,
        compiler_params=pltpu.CompilerParams(
            collective_id=0, has_side_effects=True, vmem_limit_bytes=56 * 2**20),
        cost_estimate=pl.CostEstimate(flops=6 * 10**9, bytes_accessed=8 * 10**6, transcendentals=10**6),
        name="train_step",
    )(tokens, embed_table, mix_weight, kernels, donor_proj, acceptor_proj, tissue_scale,
      junction_dest.reshape(1, J), donor_offset, acceptor_offset, tissue_ids, targets)
    feat, igrad, *rest = res
    return (feat[None], igrad[None], *rest)


def solution(mesh):
    s = P("dp", "seq")
    placed = (s, P(), P(), P(), P(), P(), P(), P("dp", "seq", None), s, s, s, s)
    return jax.shard_map(
        per_device,
        mesh=mesh,
        in_specs=placed,
        out_specs=(P("dp", "seq", None), P("dp", "seq", None), P(None, "dp", None), P(None, None, "dp"),
                   P(None, "dp"), P("dp", None), P("dp", None), P(None, "dp")),
        check_vma=False,
    )
```

time: 414 us -> 72.8 us (0.18)
  waiting for transfers between devices: 188 us -> 0 us
  local copies, waits for them, and re-layouts: 98.6 us -> 9.84 us
  Pallas kernels: 0 us -> 62 us
  starting transfers between devices: 35.4 us -> 0 us
  matrix products: 25.8 us -> 0 us
  other arithmetic: 25.1 us -> 0 us
  blocking collectives: 23.4 us -> 0 us
  between operations: 15.1 us -> 0.66 us
    reduce_scatter x3 -> x0, waiting for transfers between devices: 79.5 us -> none  [the longest x1 79.4 us: per_device(): lax.psum_scatter(summed_output[0], 'dp', scatter_dimension=1, tiled=True)]
    scatter x2 -> x0, local copies, waits for them, and re-layouts: 68.3 us -> none  [the longest x1 38.7 us: per_device(): jnp.full((count, capacity), -1, jnp.int32).at[dest, slot].set(accept_rows)]
    pallas_call x0 -> x1, Pallas kernels: none -> 62 us  [per_device(): pl.pallas_call(functools.partial(body, (n, m, L, J, C, E, cap, V)), out_s...]
    unnamed x10 -> x0, waiting for transfers between devices: 60.9 us -> none
    psum x1 -> x0, waiting for transfers between devices: 36.5 us -> none  [per_device(): lax.psum((mix_local, donor_part, accept_part, kernel_local, embed_part, t...]
    psum x1 -> x0, blocking collectives: 23.4 us -> none  [per_device(): lax.psum((mix_local, donor_part, accept_part, kernel_local, embed_part, t...]
    dot_general x14 -> x0, matrix products: 22.4 us -> none  [the longest x2 6.05 us: per_device(): jnp.dot(upstream_low, mix_weight[layer_index].T, preferred_element_type=j...]
    ppermute x8 -> x0, starting transfers between devices: 17.6 us -> none  [the longest x4 12.3 us: padded(): lax.ppermute(tail, axis, [(i, (i + 1) % count) for i in range(ends)])]
  transfers between devices with their start and end apart: 18 -> 0, of which waited for: 9 -> 0; matrix products, arithmetic and copies ran while one was open for 20% -> 0% of each run, Pallas kernels for 0% -> 0%
where the time goes in v1:
time: 72.8 us; the launch traced here: 72.5 us
  Pallas kernels  62 us (85%)
  local copies, waits for them, and re-layouts  9.84 us (14%)
    pallas_call x1, Pallas kernels, per_device(): pl.pallas_call(functools.partial(body, (n, m, L, J, C, E, cap, V)), out_s...  62 us
    unnamed x21, local copies, waits for them, and re-layouts  9.84 us

profile of v1, /device:TPU:0, one launch (start us, length us, event | category | flops | bytes accessed | tf_op | source)
XLA Modules:
  0.0 72.5 jit_solution(1106716465909503593)
XLA Ops:
  0.6 1.3 %copy.20.refs_3_ = bf16[2,3,768]{2,1,0:T(4,128)(2,1)} copy(bf16[2,3,768]{2,0,1:T(2,128)(2,1)} %param.15) | data formatting | bytes 18432 | tf_op args[3]
  1.9 62.0 %train_step.1 = (bf16[512,768]{1,0:T(8,128)(2,1)}, bf16[512,768]{1,0:T(8,128)(2,1)}, f32[2,192,768]{2,1,0:T(8,128)}, f32[2,3,192]{2,1,0:T(4,128)}, f32[4,192]{1,...) custom-call(s32[1,512]{1,0:T(1,128)} %refs_0_.1, bf16[4,768]{1,0:T(4,128)(2,1)} %refs_1_.1, ...), custom_call_target="tpu_custom_call" | custom-call | flops 6000000000 | bytes 8000000 | tf_op jit(solution)/shard_map/train_step/pallas_call | solution.py:465
  63.9 0.0 copy-start.1
  63.9 1.4 %copy.21 = f32[2,3,192]{2,0,1:T(2,128)} copy(f32[2,3,192]{2,1,0:T(4,128)} %get-tuple-element.27) | data formatting | bytes 9216
  65.3 2.1 %copy.29 = bf16[1,512,768]{2,1,0:T(8,128)(2,1)} copy(bf16[1,512,768]{2,1,0:T(8,128)(2,1)} %bitcast.4) | data formatting | bytes 1572864
  67.4 0.0 copy-done.1
  67.4 0.0 copy-start
  67.4 0.9 %copy.30 = bf16[1,512,768]{2,1,0:T(8,128)(2,1)} copy(bf16[1,512,768]{2,1,0:T(8,128)(2,1)S(1)} %bitcast.3) | data formatting | bytes 1572864
  68.2 0.7 copy-done
  68.9 0.0 copy-start.4
  68.9 0.0 copy-start.3
  68.9 0.0 copy-start.2
  68.9 0.0 copy-start.5
  68.9 1.0 %copy.31 = f32[2,192,768]{2,1,0:T(8,128)} copy(f32[2,192,768]{2,1,0:T(8,128)S(1)} %copy-done) | data formatting | bytes 2359296
  69.9 0.0 copy-done.4
  70.0 0.6 copy.32
  70.5 0.0 copy-done.3
  70.5 0.7 copy.33
  71.2 0.0 copy-done.2
  71.2 0.7 copy.34
  71.9 0.0 copy-done.5
  71.9 0.6 copy.35
Async XLA Ops:
  63.9 3.4 %copy-start.1 = (bf16[512,768]{1,0:T(8,128)(2,1)S(1)}, bf16[512,768]{1,0:T(8,128)(2,1)}, u32[]{:S(2)}) copy-start(bf16[512,768]{1,0:T(8,128)(2,1)} %get-tuple-element.17) | copy-start | bytes 2359300
  67.4 1.6 %copy-start = (f32[2,192,768]{2,1,0:T(8,128)S(1)}, f32[2,192,768]{2,1,0:T(8,128)}, u32[]{:S(2)}) copy-start(f32[2,192,768]{2,1,0:T(8,128)} %get-tuple-element.42) | copy-start | bytes 3538948
  68.9 1.0 %copy-start.4 = (f32[4,192]{1,0:T(4,128)S(1)}, f32[4,192]{1,0:T(4,128)}, u32[]{:S(2)}) copy-start(f32[4,192]{1,0:T(4,128)} %get-tuple-element.44) | copy-start | bytes 9220
  68.9 1.6 %copy-start.3 = (f32[192,256]{1,0:T(8,128)S(1)}, f32[192,256]{1,0:T(8,128)}, u32[]{:S(2)}) copy-start(f32[192,256]{1,0:T(8,128)} %get-tuple-element.45) | copy-start | bytes 589828
  68.9 2.3 %copy-start.2 = (f32[192,256]{1,0:T(8,128)S(1)}, f32[192,256]{1,0:T(8,128)}, u32[]{:S(2)}) copy-start(f32[192,256]{1,0:T(8,128)} %get-tuple-element.46) | copy-start | bytes 589828
  68.9 3.0 %copy-start.5 = (f32[4,64]{1,0:T(4,128)S(1)}, f32[4,64]{1,0:T(4,128)}, u32[]{:S(2)}) copy-start(f32[4,64]{1,0:T(4,128)} %get-tuple-element.47) | copy-start | bytes 3076

commit v2 on v1

--- a/solution.py
+++ b/solution.py
@@ -46,11 +46,15 @@
 
 def body(dims, *refs):
     n, m, L, J, C, E, cap, V = dims
-    (tok, emb, mix, kern, dproj, aproj, tscale, dest, doff, aoff, tissue, targets) = refs[:12]
-    (feat, igrad, mixg, kerng, embg, dong, accg, tisg) = refs[12:20]
+    (tok, emb, mix_in, kern, dproj, aproj, tscale, dest, doff, aoff, tissue, targets) = refs[:12]
+    (feat_out, igrad, mixg, kerng, embg, dong, accg, tisg) = refs[12:20]
     (info_src, info_all, x1, n1e, act, gp1, G, Dm, ans, ret, bb, gq, A, g2, da, dc1e, g1, dc0e,
      gp0, n0l, n0c, n0r, acttT, mt, oh, ohT, n0g, gp0g, inv0g,
-     pay, rc, chip, rj, ck, rz, F, sp, rs, s1, rsz, sall, ssem, rsem) = refs[20:]
+     pay, rc, chip, rj, ck, rz, F, sp, rs, s1, rsz, sall, ssem, rsem, mix, feat, lsem) = refs[20:]
+    loads = [pltpu.make_async_copy(mix_in.at[i], mix.at[i], lsem.at[i]) for i in range(2)]
+    for cp in loads:
+        cp.start()
+    store = pltpu.make_async_copy(feat, feat_out, lsem.at[2])
     me = lax.axis_index("seq")
     q = lax.axis_index("dp")
     groups = n // GROUP
@@ -100,15 +104,31 @@
     info_src[1:2, :J] = dest[...]
     info_src[1:2, J:2 * J] = aoff[...]
     info_all[me] = info_src[...]
+    upper = onehot(lax.broadcasted_iota(jnp.int32, (J, J), 0) < lax.broadcasted_iota(jnp.int32, (J, J), 1))
+    eye = lax.broadcasted_iota(jnp.int32, (J, J), 0) == lax.broadcasted_iota(jnp.int32, (J, J), 1)
+
+    def col(row):
+        return jnp.sum(jnp.where(eye, row, 0.0), axis=1, keepdims=True)
+
+    mine = lax.broadcasted_iota(jnp.int32, (n, J), 0) == dest[...]
+    before = mm(onehot(mine), upper)
+    slot = jnp.sum(jnp.where(mine, before, 0.0), axis=0, keepdims=True)
+    place = dest[...].astype(F32) * float(cap) + slot
+    Dm[...] = onehot(lax.broadcasted_iota(jnp.int32, (n * cap, J), 0).astype(F32) == place)
+    OHd = onehot(lax.broadcasted_iota(jnp.int32, (L, J), 0) == doff[...])
+    tcol = col(tissue[...].astype(F32))
+    ycol = col(targets[...])
+
     pl.semaphore_wait(barrier, count)
     info_cp = [send(info_src, info_all.at[me], q, seq_peer(k)) for k in range(1, n)]
 
+    loads[0].wait()
     ew = emb[...].astype(F32)
     inv0 = lax.rsqrt(jnp.mean(ew * ew, axis=-1, keepdims=True) + EPS)
     norm0 = ew * inv0
     n0 = norm0.astype(BF16).astype(F32)
-    k0 = kern[0].astype(F32)
-    k1 = kern[1].astype(F32)
+    k0 = jnp.concatenate([kern[k].astype(F32)[0:1] for k in range(3)], axis=0)
+    k1 = jnp.concatenate([kern[k].astype(F32)[1:2] for k in range(3)], axis=0)
     idf = lax.broadcasted_iota(jnp.int32, (COMBOS, 1), 0).astype(F32)
     cc = jnp.floor((idf + 0.5) * (1.0 / 25.0))
     rest = idf - 25.0 * cc
@@ -139,21 +159,6 @@
     mt[:, :C] = x1t
     mt[:, C:2 * C] = n1t
 
-    upper = onehot(lax.broadcasted_iota(jnp.int32, (J, J), 0) < lax.broadcasted_iota(jnp.int32, (J, J), 1))
-    eye = lax.broadcasted_iota(jnp.int32, (J, J), 0) == lax.broadcasted_iota(jnp.int32, (J, J), 1)
-
-    def col(row):
-        return jnp.sum(jnp.where(eye, row, 0.0), axis=1, keepdims=True)
-
-    mine = lax.broadcasted_iota(jnp.int32, (n, J), 0) == dest[...]
-    before = mm(onehot(mine), upper)
-    slot = jnp.sum(jnp.where(mine, before, 0.0), axis=0, keepdims=True)
-    place = dest[...].astype(F32) * float(cap) + slot
-    Dm[...] = onehot(lax.broadcasted_iota(jnp.int32, (n * cap, J), 0).astype(F32) == place)
-    OHd = onehot(lax.broadcasted_iota(jnp.int32, (L, J), 0) == doff[...])
-    tcol = col(tissue[...].astype(F32))
-    ycol = col(targets[...])
-
     for cp in info_cp:
         cp.wait_recv()
     lt = jnp.where(me == 0, V, info_all[lax.rem(me + n - 1, n)][0:1, :L])
@@ -182,10 +187,12 @@
         act[pl.ds(r, R)] = a.astype(BF16)
         gp1[pl.ds(r, R)] = s
 
+    loads[1].wait()
     for h in range(2):
         sl = slice(h * L // 2, (h + 1) * L // 2)
         feat[sl] = (x1[sl].astype(F32) + mm(act[sl], mix[1])).astype(BF16)
 
+    store.start()
     rows = [info_all[s][1:2, :] for s in range(n)]
     dests = jnp.concatenate([r[:, :J] for r in rows], axis=0)
     hits = dests == me
@@ -228,14 +235,52 @@
             for t in range(tscale.shape[0])]
     g2[...] = mm_tb(A[:, :E], dproj[...])
 
+    hq = rows_q // 2
+
     def weights_half(h):
         a = A[:, h * E:(h + 1) * E]
-        for which, left in ((0, act), (4, feat)):
+        for which, left in ((0, act), (1, feat)):
             out = mm_ta(left[...], a).astype(BF16)
-            for c in range(E // 128):
-                pay[which + h * (E // 128) + c] = out[:, c * 128:(c + 1) * 128]
-
-    weights_half(0)
+            for c in range(2):
+                for b in range(2):
+                    for i in range(m):
+                        pay[h, b, which * 2 + c, i * hq:(i + 1) * hq] = out[
+                            i * rows_q + b * hq:i * rows_q + (b + 1) * hq, c * 128:(c + 1) * 128]
+        return send(pay.at[h, 1 - b0], rc.at[h], q, me + 1 - 2 * b0)
+
+    def chip_stage(h, cp):
+        cp.wait_recv()
+        for j in range(4):
+            chip[h, j] = (pay[h, b0, j].astype(F32) + rc[h, j].astype(F32)).astype(BF16)
+        out = []
+        for k in range(1, 4):
+            jj = lax.rem(j0 + k, 4)
+            out.append(send(chip.at[h, jj], rj.at[h, k - 1], q, base + jj * 2 + b0))
+        return out
+
+    def z_stage(h, cps):
+        for cp in cps:
+            cp.wait_recv()
+        ck[h] = (chip[h, j0].astype(F32) + rj[h, 0].astype(F32) + rj[h, 1].astype(F32)
+                 + rj[h, 2].astype(F32)).astype(BF16)
+        out = []
+        for k in range(1, T):
+            pq, pg = t_peer(k)
+            out.append(send(ck.at[h, pl.ds(pl.multiple_of(pq * hq, 16), hq)], rz.at[h, k - 1],
+                            pq, pg * GROUP + low))
+        return out
+
+    def gather_stage(h, cps):
+        for cp in cps:
+            cp.wait_recv()
+        tot = ck[h, pl.ds(pl.multiple_of(q * hq, 16), hq)].astype(F32)
+        for k in range(T - 1):
+            tot = tot + rz[h, k].astype(F32)
+        p0 = b0 * 4 + j0
+        F[h, p0] = tot.astype(BF16)
+        return [send(F.at[h, p0], F.at[h, p0], q, base + low_peer(k)) for k in range(1, GROUP)]
+
+    core0 = weights_half(0)
 
     for cp in back_cp:
         cp.wait_recv()
@@ -253,8 +298,8 @@
         send(dc1e.at[pl.ds(L, D1)], dc1e.at[pl.ds(0, D1)], q, seq_peer(1)),
         send(dc1e.at[pl.ds(D1, D1)], dc1e.at[pl.ds(L + D1, D1)], q, seq_peer(n - 1)),
     ]
-    weights_half(1)
-    core_cp = send(pay.at[pl.ds((1 - b0) * 4, 4)], rc, q, me + 1 - 2 * b0)
+    chip0 = chip_stage(0, core0)
+    core1 = weights_half(1)
     pl.loop(D1 // R, (L - D1) // R)(slope_times)
 
     def kg(i, accs):
@@ -270,6 +315,7 @@
     tail = [jnp.concatenate([t, jnp.zeros((1, C - E), F32)], axis=1) for t in tail]
     extra = jnp.concatenate(kacc + [zc] + tail + [zc] * 8, axis=0)
 
+    chip1 = chip_stage(1, core1)
     for cp in halo_cp:
         cp.wait_recv()
 
@@ -298,14 +344,7 @@
     sp[7] = extra.astype(BF16)
     srs_cp = [send(sp.at[low_peer(k)], rs.at[k - 1], q, base + low_peer(k)) for k in range(1, GROUP)]
 
-    core_cp.wait_recv()
-    for j in range(4):
-        chip[j] = (pay[b0 * 4 + j].astype(F32) + rc[j].astype(F32)).astype(BF16)
-    chip_cp = []
-    for k in range(1, 4):
-        jj = lax.rem(j0 + k, 4)
-        chip_cp.append(send(chip.at[jj], rj.at[k - 1], q, base + jj * 2 + b0))
-
+    z0 = z_stage(0, chip0)
     da[...] = mm_tb(g1[...].astype(BF16), mix[0])
 
     def slope0(i):
@@ -331,13 +370,8 @@
         pq, pg = t_peer(k)
         sz_cp.append(send(s1, rsz.at[k - 1], pq, pg * GROUP + low))
 
-    for cp in chip_cp:
-        cp.wait_recv()
-    ck[...] = (chip[j0].astype(F32) + rj[0].astype(F32) + rj[1].astype(F32) + rj[2].astype(F32)).astype(BF16)
-    z_cp = []
-    for k in range(1, T):
-        pq, pg = t_peer(k)
-        z_cp.append(send(ck.at[pl.ds(pl.multiple_of(pq * rows_q, 16), rows_q)], rz.at[k - 1], pq, pg * GROUP + low))
+    z1 = z_stage(1, chip1)
+    ag0 = gather_stage(0, z0)
 
     for cp in halo0_cp:
         cp.wait_recv()
@@ -358,14 +392,7 @@
     sall[low] = tot.astype(BF16)
     sag_cp = [send(sall.at[low], sall.at[low], q, base + low_peer(k)) for k in range(1, GROUP)]
 
-    for cp in z_cp:
-        cp.wait_recv()
-    tot = ck[pl.ds(pl.multiple_of(q * rows_q, 16), rows_q)].astype(F32)
-    for k in range(T - 1):
-        tot = tot + rz[k].astype(F32)
-    p0 = b0 * 4 + j0
-    F[p0] = tot.astype(BF16)
-    ag_cp = [send(F.at[p0], F.at[p0], q, base + low_peer(k)) for k in range(1, GROUP)]
+    ag1 = gather_stage(1, z1)
 
     @pl.loop(0, L // R)
     def _(i):
@@ -397,9 +424,11 @@
 
     kg0 = jnp.concatenate(
         [jnp.sum(t[...] * Tm, axis=0, keepdims=True) for t in (n0l, n0c, n0r)], axis=0)
-    kerng[0] = own(kg0, C)
     last = sall[7].astype(F32)
-    kerng[1] = own(last[0:3], C)
+    kg0 = own(kg0, C)
+    kg1 = own(last[0:3], C)
+    for k in range(3):
+        kerng[k] = jnp.concatenate([kg0[k:k + 1], kg1[k:k + 1]], axis=0)
     tisg[...] = own(last[4:4 + tscale.shape[0], :E], E)
     eg = []
     for v in range(V):
@@ -410,17 +439,32 @@
         eg.append(total(cc, Sm) + inv0[v:v + 1] * (D - nv * jnp.mean(D * nv, axis=-1, keepdims=True)))
     embg[...] = own(jnp.concatenate(eg, axis=0), C)
 
-    for cp in ag_cp:
-        cp.wait_recv()
-    half = E // 128
-    md = jnp.concatenate([F[i] for i in range(half)], axis=1)
-    ma = jnp.concatenate([F[half + i] for i in range(half)], axis=1)
-    mixg[1] = mm_tb(md, dproj[...]) + mm_tb(ma, aproj[...])
-    for i in range(half):
-        dong[:, i * 128:(i + 1) * 128] = F[4 + i].astype(F32)
-        accg[:, i * 128:(i + 1) * 128] = F[4 + half + i].astype(F32)
+    for cp in ag0 + ag1:
+        cp.wait_recv()
+    for b in range(2):
+        sl = slice(b * hq, (b + 1) * hq)
+        md = jnp.concatenate([F[0, b * 4], F[0, b * 4 + 1]], axis=1)
+        ma = jnp.concatenate([F[1, b * 4], F[1, b * 4 + 1]], axis=1)
+        mixg[1, sl] = mm_tb(md, dproj[...]) + mm_tb(ma, aproj[...])
+        for c in range(2):
+            dong[sl, c * 128:(c + 1) * 128] = F[0, b * 4 + 2 + c].astype(F32)
+            accg[sl, c * 128:(c + 1) * 128] = F[1, b * 4 + 2 + c].astype(F32)
+    store.wait()
     for cp in sent:
         cp.wait_send()
+
+
+def hand_over(*refs):
+    held, sem = refs[16:24], refs[24]
+    ins = [pltpu.make_async_copy(refs[i], held[i], sem.at[0, i]) for i in range(8)]
+    outs = [pltpu.make_async_copy(held[i], refs[8 + i], sem.at[1, i]) for i in range(8)]
+    for cp in ins:
+        cp.start()
+    for i in range(8):
+        ins[i].wait()
+        outs[i].start()
+    for cp in outs:
+        cp.wait()
 
 
 def per_device(tokens, embed_table, mix_weight, kernels, donor_proj, acceptor_proj, tissue_scale,
@@ -437,7 +481,7 @@
     rq = C // m
     W = L + 2 * D1
     vm = pltpu.VMEM
-    nsem = 3 * (n - 1) + 4 + 1 + 3 + 2 * (T - 1) + 3 * (GROUP - 1)
+    nsem = 3 * (n - 1) + 4 + 2 * (1 + 3) + 3 * (T - 1) + 4 * (GROUP - 1)
     scratch = [
         vm((8, max(L, 2 * J)), jnp.int32), vm((n, 8, max(L, 2 * J)), jnp.int32),
         vm((L, C), BF16), vm((W, C), BF16), vm((L, C), BF16), vm((L, C), F32),
@@ -449,33 +493,46 @@
         vm((C, COMBOS), BF16), vm((COMBOS, 2 * C), BF16),
         vm((W, COMBOS), BF16), vm((COMBOS, W), BF16),
         vm((L, C), BF16), vm((L, C), BF16), vm((L, 128), F32),
-        vm((8, C, 128), BF16), vm((4, C, 128), BF16), vm((4, C, 128), BF16), vm((3, C, 128), BF16),
-        vm((C, 128), BF16), vm((T - 1, rq, 128), BF16), vm((8, rq, 128), BF16),
+        vm((2, 2, 4, C // 2, 128), BF16), vm((2, 4, C // 2, 128), BF16), vm((2, 4, C // 2, 128), BF16),
+        vm((2, 3, C // 2, 128), BF16), vm((2, C // 2, 128), BF16), vm((2, T - 1, rq // 2, 128), BF16),
+        vm((2, 8, rq // 2, 128), BF16),
         vm((8, 16, C), BF16), vm((7, 16, C), BF16), vm((16, C), BF16), vm((T - 1, 16, C), BF16),
         vm((8, 16, C), BF16),
         pltpu.SemaphoreType.DMA((nsem,)), pltpu.SemaphoreType.DMA((nsem,)),
+        vm((2, C, C), BF16), vm((L, C), BF16), pltpu.SemaphoreType.DMA((3,)),
     ]
     outs = [
         jax.ShapeDtypeStruct((L, C), BF16), jax.ShapeDtypeStruct((L, C), BF16),
-        jax.ShapeDtypeStruct((2, rq, C), F32), jax.ShapeDtypeStruct((2, 3, rq), F32),
+        jax.ShapeDtypeStruct((2, rq, C), F32), jax.ShapeDtypeStruct((3, 2, rq), F32),
         jax.ShapeDtypeStruct((V, rq), F32), jax.ShapeDtypeStruct((rq, E), F32),
         jax.ShapeDtypeStruct((rq, E), F32), jax.ShapeDtypeStruct((tissue_scale.shape[0], E // m), F32),
     ]
     spec = pl.BlockSpec(memory_space=pltpu.VMEM)
+    anywhere = pl.BlockSpec(memory_space=pl.ANY)
     res = pl.pallas_call(
         functools.partial(body, (n, m, L, J, C, E, cap, V)),
         out_shape=outs,
-        in_specs=[spec] * 12,
-        out_specs=[spec] * 8,
+        in_specs=[spec] * 2 + [anywhere] + [spec] * 9,
+        out_specs=[anywhere] + [spec] * 7,
         scratch_shapes=scratch,
         compiler_params=pltpu.CompilerParams(
             collective_id=0, has_side_effects=True, vmem_limit_bytes=56 * 2**20),
         cost_estimate=pl.CostEstimate(flops=6 * 10**9, bytes_accessed=8 * 10**6, transcendentals=10**6),
         name="train_step",
-    )(tokens, embed_table, mix_weight, kernels, donor_proj, acceptor_proj, tissue_scale,
+    )(tokens, embed_table, mix_weight, kernels.transpose(1, 0, 2), donor_proj, acceptor_proj, tissue_scale,
       junction_dest.reshape(1, J), donor_offset, acceptor_offset, tissue_ids, targets)
-    feat, igrad, *rest = res
-    return (feat[None], igrad[None], *rest)
+    res = pl.pallas_call(
+        hand_over,
+        out_shape=outs,
+        in_specs=[anywhere] * 8,
+        out_specs=[anywhere] * 8,
+        scratch_shapes=[vm(o.shape, o.dtype) for o in outs] + [pltpu.SemaphoreType.DMA((2, 8))],
+        compiler_params=pltpu.CompilerParams(vmem_limit_bytes=16 * 2**20),
+        cost_estimate=pl.CostEstimate(flops=0, bytes_accessed=6 * 10**6, transcendentals=0),
+        name="hand_over",
+    )(*res)
+    feat, igrad, mixg, kerng, *rest = res
+    return (feat[None], igrad[None], mixg, kerng.transpose(1, 0, 2), *rest)
 
 
 def solution(mesh):

time: 72.8 us -> 67 us (0.920)
  Pallas kernels: 62 us -> 58.5 us
  local copies, waits for them, and re-layouts: 9.84 us -> 7.42 us
    pallas_call x1, Pallas kernels: 62 us -> 55.9 us  [per_device(): pl.pallas_call(functools.partial(body, (n, m, L, J, C, E, cap, V)), out_s...]
    pallas_call x0 -> x1, Pallas kernels: none -> 2.65 us  [per_device(): pl.pallas_call(hand_over, out_shape=outs, in_specs=[anywhere] * 8, out_sp...]
    unnamed x21 -> x16, local copies, waits for them, and re-layouts: 9.84 us -> 7.42 us
where the time goes in v2:
time: 67 us; the launch traced here: 66.6 us
  Pallas kernels  58.5 us (87%)
  local copies, waits for them, and re-layouts  7.42 us (11%)
    pallas_call x1, Pallas kernels, per_device(): pl.pallas_call(functools.partial(body, (n, m, L, J, C, E, cap, V)), out_s...  55.9 us
    unnamed x16, local copies, waits for them, and re-layouts  7.42 us
    pallas_call x1, Pallas kernels, per_device(): pl.pallas_call(hand_over, out_shape=outs, in_specs=[anywhere] * 8, out_sp...  2.65 us

profile of v2, /device:TPU:0, one launch (start us, length us, event | category | flops | bytes accessed | tf_op | source)
XLA Modules:
  0.0 66.6 jit_solution(3946311659980111969)
XLA Ops:
  0.6 55.9 %train_step.1 = (bf16[512,768]{1,0:T(8,128)(2,1)}, bf16[512,768]{1,0:T(8,128)(2,1)}, f32[2,192,768]{2,1,0:T(8,128)}, f32[3,2,192]{2,1,0:T(2,128)}, f32[4,192]{1,...) custom-call(s32[1,512]{1,0:T(1,128)} %refs_0_.1, bf16[4,768]{1,0:T(4,128)(2,1)} %refs_1_.1, ...), custom_call_target="tpu_custom_call" | custom-call | flops 6000000000 | bytes 8000000 | tf_op jit(solution)/shard_map/train_step/pallas_call | solution.py:512
  56.5 0.0 copy-start
  56.5 1.3 %copy-done = f32[2,192,768]{2,1,0:T(8,128)S(1)} copy-done((f32[2,192,768]{2,1,0:T(8,128)S(1)}, f32[2,192,768]{2,1,0:T(8,128)}, u32[]{:S(2)}) %copy-start) | copy-done | bytes 1179672
  57.8 0.0 copy-start.1
  57.8 1.1 %copy-done.1 = bf16[512,768]{1,0:T(8,128)(2,1)S(1)} copy-done((bf16[512,768]{1,0:T(8,128)(2,1)S(1)}, bf16[512,768]{1,0:T(8,128)(2,1)}, u32[]{:S(2)}) %copy-start.1) | copy-done | bytes 786456
  58.9 0.0 copy-start.2
  58.9 1.1 %copy-done.2 = bf16[512,768]{1,0:T(8,128)(2,1)S(1)} copy-done((bf16[512,768]{1,0:T(8,128)(2,1)S(1)}, bf16[512,768]{1,0:T(8,128)(2,1)}, u32[]{:S(2)}) %copy-start.2) | copy-done | bytes 786456
  60.1 0.0 copy-start.3
  60.1 0.9 %copy-done.3 = f32[192,256]{1,0:T(8,128)S(1)} copy-done((f32[192,256]{1,0:T(8,128)S(1)}, f32[192,256]{1,0:T(8,128)}, u32[]{:S(2)}) %copy-start.3) | copy-done | bytes 196632
  61.0 0.0 copy-start.4
  61.0 0.9 %copy-done.4 = f32[192,256]{1,0:T(8,128)S(1)} copy-done((f32[192,256]{1,0:T(8,128)S(1)}, f32[192,256]{1,0:T(8,128)}, u32[]{:S(2)}) %copy-start.4) | copy-done | bytes 196632
  61.9 0.0 copy-start.5
  61.9 0.7 %copy-done.5 = f32[3,2,192]{2,1,0:T(2,128)S(1)} copy-done((f32[3,2,192]{2,1,0:T(2,128)S(1)}, f32[3,2,192]{2,1,0:T(2,128)}, u32[]{:S(2)}) %copy-start.5) | copy-done | bytes 4632
  62.6 0.0 copy-start.6
  62.6 0.7 %copy-done.6 = f32[4,192]{1,0:T(4,128)S(1)} copy-done((f32[4,192]{1,0:T(4,128)S(1)}, f32[4,192]{1,0:T(4,128)}, u32[]{:S(2)}) %copy-start.6) | copy-done | bytes 3096
  63.3 0.0 copy-start.7
  63.3 0.7 copy-done.7
  64.0 2.7 %hand_over.1 = (bf16[512,768]{1,0:T(8,128)(2,1)}, bf16[512,768]{1,0:T(8,128)(2,1)}, f32[2,192,768]{2,1,0:T(8,128)}, f32[3,2,192]{2,1,0:T(2,128)}, f32[4,192]{1,0...) custom-call(bf16[512,768]{1,0:T(8,128)(2,1)S(1)} %copy-done.1, ...), custom_call_target="tpu_custom_call" | custom-call | bytes 6000000 | tf_op jit(solution)/shard_map/hand_over/pallas_call | solution.py:524
Async XLA Ops:
  56.5 1.3 %copy-start = (f32[2,192,768]{2,1,0:T(8,128)S(1)}, f32[2,192,768]{2,1,0:T(8,128)}, u32[]{:S(2)}) copy-start(f32[2,192,768]{2,1,0:T(8,128)} %get-tuple-element.26.refs_2_) | copy-start | bytes 3538948
  57.8 1.1 %copy-start.1 = (bf16[512,768]{1,0:T(8,128)(2,1)S(1)}, bf16[512,768]{1,0:T(8,128)(2,1)}, u32[]{:S(2)}) copy-start(bf16[512,768]{1,0:T(8,128)(2,1)} %get-tuple-element.24.refs_0_) | copy-start | bytes 2359300
  58.9 1.1 %copy-start.2 = (bf16[512,768]{1,0:T(8,128)(2,1)S(1)}, bf16[512,768]{1,0:T(8,128)(2,1)}, u32[]{:S(2)}) copy-start(bf16[512,768]{1,0:T(8,128)(2,1)} %get-tuple-element.25.refs_1_) | copy-start | bytes 2359300
  60.1 0.9 %copy-start.3 = (f32[192,256]{1,0:T(8,128)S(1)}, f32[192,256]{1,0:T(8,128)}, u32[]{:S(2)}) copy-start(f32[192,256]{1,0:T(8,128)} %get-tuple-element.29.refs_5_) | copy-start | bytes 589828
  61.0 0.9 %copy-start.4 = (f32[192,256]{1,0:T(8,128)S(1)}, f32[192,256]{1,0:T(8,128)}, u32[]{:S(2)}) copy-start(f32[192,256]{1,0:T(8,128)} %get-tuple-element.30.refs_6_) | copy-start | bytes 589828
  61.9 0.7 %copy-start.5 = (f32[3,2,192]{2,1,0:T(2,128)S(1)}, f32[3,2,192]{2,1,0:T(2,128)}, u32[]{:S(2)}) copy-start(f32[3,2,192]{2,1,0:T(2,128)} %get-tuple-element.27.refs_3_) | copy-start | bytes 13828
  62.6 0.7 %copy-start.6 = (f32[4,192]{1,0:T(4,128)S(1)}, f32[4,192]{1,0:T(4,128)}, u32[]{:S(2)}) copy-start(f32[4,192]{1,0:T(4,128)} %get-tuple-element.28.refs_4_) | copy-start | bytes 9220
  63.3 0.7 copy-start.7

commit v3 on v2

--- a/solution.py
+++ b/solution.py
@@ -527,7 +527,7 @@
         in_specs=[anywhere] * 8,
         out_specs=[anywhere] * 8,
         scratch_shapes=[vm(o.shape, o.dtype) for o in outs] + [pltpu.SemaphoreType.DMA((2, 8))],
-        compiler_params=pltpu.CompilerParams(vmem_limit_bytes=16 * 2**20),
+        compiler_params=pltpu.CompilerParams(vmem_limit_bytes=56 * 2**20),
         cost_estimate=pl.CostEstimate(flops=0, bytes_accessed=6 * 10**6, transcendentals=0),
         name="hand_over",
     )(*res)

time: 67 us -> 59.7 us (0.89)
  local copies, waits for them, and re-layouts: 7.42 us -> 0 us
    unnamed x16 -> x0, local copies, waits for them, and re-layouts: 7.42 us -> none
where the time goes in v3:
time: 59.7 us; the launch traced here: 59.5 us
  Pallas kernels  58.9 us (99%)
  between operations  0.65 us (1%)
    pallas_call x1, Pallas kernels, per_device(): pl.pallas_call(functools.partial(body, (n, m, L, J, C, E, cap, V)), out_s...  55.9 us
    pallas_call x1, Pallas kernels, per_device(): pl.pallas_call(hand_over, out_shape=outs, in_specs=[anywhere] * 8, out_sp...  3.03 us

profile of v3, /device:TPU:0, one launch (start us, length us, event | category | flops | bytes accessed | tf_op | source)
XLA Modules:
  0.0 59.5 jit_solution(17602531632887646384)
XLA Ops:
  0.6 55.9 %train_step.1 = (bf16[512,768]{1,0:T(8,128)(2,1)}, bf16[512,768]{1,0:T(8,128)(2,1)}, f32[2,192,768]{2,1,0:T(8,128)}, f32[3,2,192]{2,1,0:T(2,128)}, f32[4,192]{1,...) custom-call(s32[1,512]{1,0:T(1,128)} %refs_0_.1, bf16[4,768]{1,0:T(4,128)(2,1)} %refs_1_.1, ...), custom_call_target="tpu_custom_call" | custom-call | flops 6000000000 | bytes 8000000 | tf_op jit(solution)/shard_map/train_step/pallas_call | solution.py:512
  56.5 3.0 %hand_over.1 = (bf16[512,768]{1,0:T(8,128)(2,1)}, bf16[512,768]{1,0:T(8,128)(2,1)}, f32[2,192,768]{2,1,0:T(8,128)}, f32[3,2,192]{2,1,0:T(2,128)}, f32[4,192]{1,0...) custom-call(bf16[512,768]{1,0:T(8,128)(2,1)} %get-tuple-element.24.refs_0_, ...), custom_call_target="tpu_custom_call" | custom-call | bytes 6000000 | tf_op jit(solution)/shard_map/hand_over/pallas_call | solution.py:524
